TPU v7x, 32 devices: a whole 2x2x4 slice. The times are simulated.
32 devices in a mesh: row: 4 (over y, core), col: 8 (over z, x).
Axes of the slice: x: 2, y: 2, z: 4, core: 2. Of those that a mesh axis runs over, the one named last changes fastest.
Arguments:
- hidden: bfloat16 [8192, 4608], P('col', 'row'), may hold values from -6 to 6
- w_query: bfloat16 [4608, 4096], P('col', 'row'), may hold values from -0.09375 to 0.09375
- w_key: bfloat16 [4608, 2048], P('col', 'row'), may hold values from -0.09375 to 0.09375
- w_value: bfloat16 [4608, 2048], P('col', 'row'), may hold values from -0.09375 to 0.09375
- adapter_down: bfloat16 [8, 4608, 32], P('col', 'row'), may hold values from -0.09375 to 0.09375
- adapter_up_query: bfloat16 [8, 16, 4096], P('col', None, 'row'), may hold values from -1.5 to 1.5
- adapter_up_value: bfloat16 [8, 16, 2048], P('col', None, 'row'), may hold values from -1.5 to 1.5
- lengths: int32 [8, 10], P('col'), may hold values from 1 to 192, 1024 in all within a row
- request_adapter: int32 [8, 10], P('col'), may hold values from 0 to 7
- adapter_slot: int32 [8], replicated, may hold values from 0 to 7, each once
- page_table: int32 [8, 18], P('col'), may hold values from 0 to 17, each once within a row
Outputs:
- query: bfloat16 [8192, 4096], P('col', 'row')
- key_cache: bfloat16 [144, 128, 2048], P('col', None, 'row')
- value_cache: bfloat16 [144, 128, 2048], P('col', None, 'row')
Inputs may be any that keep to these rules, and one draw needn't show every extreme that they name: Each row of lengths sums to 1024, and its longest request has exactly 192 tokens. `adapter_slot`: a permutation of the slots. `page_table`: each row is a permutation of the 18 local slots.
All inputs are finite; a program needn't handle non-finite values.
Results may differ from a plain program's by a relative error of at most 0.0039.
Values may be sent and summed in bfloat16 or wider, within the bound.
A program may use at most 128 MiB of HBM per device.

v0:
```python
import math

import jax
import jax.numpy as jnp
from jax import lax
from jax.sharding import PartitionSpec as P

HEAD = 128
PAGE = 128
MOST = 192
TOK_DEV = 1024


def rotate(values, position):
    half_width = HEAD // 2
    frequency = jnp.exp(
        jnp.arange(half_width, dtype=jnp.float32) * (-2.0 * math.log(10000.0) / HEAD)
    )
    angles = position.astype(jnp.float32)[:, None] * frequency[None, :]
    cosine = jnp.cos(angles)[:, None, :]
    sine_value = jnp.sin(angles)[:, None, :]
    shaped = values.reshape(values.shape[0], -1, HEAD)
    leading = shaped[:, :, :half_width]
    second = shaped[:, :, half_width:]
    rotated = jnp.concatenate(
        [leading * cosine - second * sine_value, second * cosine + leading * sine_value], axis=2
    )
    return rotated.reshape(values.shape)


def layout(lengths, page_row):
    token_index = jnp.arange(TOK_DEV, dtype=jnp.int32)
    starts = jnp.cumsum(lengths) - lengths
    request_of = jnp.sum((token_index[:, None] >= starts[None, :]).astype(jnp.int32), axis=1) - 1
    position = token_index - jnp.take(starts, request_of)
    pages_each = (lengths + PAGE - 1) // PAGE
    page_start = jnp.cumsum(pages_each) - pages_each
    page_index = jnp.take(page_start, request_of) + position // PAGE
    target = jnp.take(page_row, page_index) * PAGE + position % PAGE
    return (starts, request_of, position, target)


def expand_up(lowrank, chosen, up_query, up_value):
    adapter_count = up_query.shape[0]
    rank_width = up_query.shape[1]
    onehot = (chosen[:, None] == jnp.arange(adapter_count, dtype=jnp.int32)[None, :]).astype(
        lowrank.dtype
    )
    spread_query = (onehot[:, :, None] * lowrank[:, None, :rank_width]).reshape(
        -1, adapter_count * rank_width
    )
    spread_value = (onehot[:, :, None] * lowrank[:, None, rank_width:]).reshape(
        -1, adapter_count * rank_width
    )
    delta_query = jnp.dot(
        spread_query,
        up_query.reshape(adapter_count * rank_width, -1),
        preferred_element_type=jnp.float32,
    )
    delta_value = jnp.dot(
        spread_value,
        up_value.reshape(adapter_count * rank_width, -1),
        preferred_element_type=jnp.float32,
    )
    return (delta_query, delta_value)


def project_down(source, down_all, starts, lengths, chosen_request):
    tokens = source.shape[0]
    padded = jnp.concatenate([source, jnp.zeros((MOST, source.shape[1]), source.dtype)], axis=0)
    result = jnp.zeros((tokens + MOST, down_all.shape[2]), jnp.float32)
    inner_rows = jnp.arange(MOST, dtype=jnp.int32)

    def one_request(number, result):
        first_row = starts[number]
        window = lax.dynamic_slice_in_dim(padded, first_row, MOST, 0)
        factor = lax.dynamic_index_in_dim(down_all, chosen_request[number], 0, keepdims=False)
        partial_sum = jnp.dot(window, factor, preferred_element_type=jnp.float32)
        inside = (inner_rows < lengths[number]).astype(jnp.float32)[:, None]
        current = lax.dynamic_slice_in_dim(result, first_row, MOST, 0)
        return lax.dynamic_update_slice_in_dim(result, current + partial_sum * inside, first_row, 0)

    result = lax.fori_loop(0, starts.shape[0], one_request, result)
    return result[:tokens]


def shards(
    hidden,
    w_query,
    w_key,
    w_value,
    adapter_down,
    adapter_up_query,
    adapter_up_value,
    lengths,
    request_adapter,
    adapter_slot,
    page_table,
):
    starts, request_of, position, target = layout(lengths[0], page_table[0])
    full_rows = lax.all_gather(hidden, "row", axis=1, tiled=True)
    base_query = jnp.dot(
        full_rows,
        lax.all_gather(w_query, "col", axis=0, tiled=True),
        preferred_element_type=jnp.float32,
    )
    base_key = jnp.dot(
        full_rows,
        lax.all_gather(w_key, "col", axis=0, tiled=True),
        preferred_element_type=jnp.float32,
    )
    base_value = jnp.dot(
        full_rows,
        lax.all_gather(w_value, "col", axis=0, tiled=True),
        preferred_element_type=jnp.float32,
    )
    up_query, up_value = (
        lax.all_gather(adapter_up_query, "col", axis=0, tiled=True),
        lax.all_gather(adapter_up_value, "col", axis=0, tiled=True),
    )
    chosen_request = jnp.take(adapter_slot, request_adapter[0])
    rows_all = lax.all_gather(adapter_down, "row", axis=1, tiled=True)
    down_all = lax.all_gather(rows_all, "col", axis=0, tiled=True)
    lowrank = project_down(full_rows, down_all, starts, lengths[0], chosen_request)
    lowrank = lowrank.astype(jnp.bfloat16)
    chosen = jnp.take(chosen_request, request_of)
    delta_query, delta_value = expand_up(lowrank, chosen, up_query, up_value)
    query = rotate(base_query + delta_query, position).astype(jnp.bfloat16)
    key_rotated = rotate(base_key, position).astype(jnp.bfloat16)
    value_rows = (base_value + delta_value).astype(jnp.bfloat16)
    pages = page_table.shape[1]
    key_width = w_key.shape[1]
    key_cache = (
        jnp.zeros((pages * PAGE, key_width), jnp.bfloat16)
        .at[target]
        .set(key_rotated)
        .reshape(pages, PAGE, key_width)
    )
    value_cache = (
        jnp.zeros((pages * PAGE, key_width), jnp.bfloat16)
        .at[target]
        .set(value_rows)
        .reshape(pages, PAGE, key_width)
    )
    return (query, key_cache, value_cache)


def solution(mesh):
    return jax.shard_map(
        shards,
        mesh=mesh,
        in_specs=(
            P("col", "row"),
            P("col", "row"),
            P("col", "row"),
            P("col", "row"),
            P("col", "row", None),
            P("col", None, "row"),
            P("col", None, "row"),
            P("col", None),
            P("col", None),
            P(),
            P("col", None),
        ),
        out_specs=(P("col", "row"), P("col", None, "row"), P("col", None, "row")),
        check_vma=False,
    )
```

profile of v0, /device:TPU:0, one launch (start us, length us, event | category | flops | bytes accessed | tf_op | source)
XLA Modules:
  0.0 461.1 jit_solution(3003100848053034347)
XLA Ops:
  8.0 0.7 all-gather.6.cloned.1.call-update
  8.8 7.9 %all_gather.26 = bf16[1,4608,32]{1,2,0:T(8,128)(2,1)} all-gather(bf16[1,1152,32]{1,2,0:T(8,128)(2,1)S(1)} %copy-done.3), channel_id=1, replica_groups=mesh['row'=4,'col'=8] {'row'}, dimensions={1}, use_global_device_ids=true | all-gather | bytes 368640 | tf_op jit(solution)/shard_map/all_gather | solution.py:122
  18.9 31.5 %all_gather.31 = bf16[8,16,512]{2,1,0:T(8,128)(2,1)S(1)} all-gather(bf16[1,16,512]{2,1,0:T(8,128)(2,1)S(1)} %copy-done.5), channel_id=1, replica_groups=mesh['row'=4,'col'=8] {'col'}, dimensions={0}, use_global_device_ids=true | all-gather | bytes 147456 | tf_op jit(solution)/shard_map/all_gather | solution.py:119
  52.5 0.7 fusion.34
  53.3 31.8 %all_gather.28 = bf16[8,16,1024]{2,1,0:T(8,128)(2,1)S(1)} all-gather(bf16[1,16,1024]{2,1,0:T(8,128)(2,1)S(1)} %copy-done.4), channel_id=1, replica_groups=mesh['row'=4,'col'=8] {'col'}, dimensions={0}, use_global_device_ids=true | all-gather | bytes 294912 | tf_op jit(solution)/shard_map/all_gather | solution.py:118
  85.2 23.9 %compare_select_fusion.1 = (s32[1024]{0:T(1024)S(1)}, pred[1024]{0:T(1024)(128)(4,1)S(1)}, pred[1024]{0:T(1024)(128)(4,1)S(1)}, pred[1024]{0:T(1024)(128)(4,1)S(...) fusion(s32[]{:T(128)} %bitcast.41, s32[]{:T(128)} %bitcast.40, ...), kind=kLoop, calls=%fused_computation.38 | loop fusion | flops 105472 | bytes 18584 | tf_op jit(solution)/shard_map/select_n | solution.py:136
  109.1 6.3 %fusion.29 = f32[1024]{0:T(1024)S(1)} fusion(pred[1024]{0:T(1024)(128)(4,1)S(1)} %get-tuple-element.198, pred[1024]{0:T(1024)(128)(4,1)S(1)} %get-tuple-element.197, pred[1024]{0:T(1024)(128)(4,1)S(1)} %get-tuple-element.196, pred[1024]{0:T(1024)(128)(4,1)S(1)} %get-tuple-element.195, pred[1024]{0:T(1024)(128)(4,1)S(1)} %get-tuple-element.194, ...), kind=kLoop, calls=%fused_computation.55 | loop fusion | flops 12288 | bytes 14376 | tf_op jit(solution)/shard_map/convert_element_type | solution.py:19
  115.4 6.3 %select_select_fusion = s32[1024]{0:T(1024)S(1)} fusion(pred[1024]{0:T(1024)(128)(4,1)S(1)} %get-tuple-element.198, pred[1024]{0:T(1024)(128)(4,1)S(1)} %get-tuple-element.197, pred[1024]{0:T(1024)(128)(4,1)S(1)} %get-tuple-element.196, pred[1024]{0:T(1024)(128)(4,1)S(1)} %get-tuple-element.195, pred[1024]{0:T(1024)(128)(4,1)S(1)} %get-tuple-element.194, ...), kind=kLoop, calls=%fused_computation.49 | loop fusion | flops 10240 | bytes 14376 | tf_op jit(solution)/shard_map/jit(_take)/select_n | solution.py:126
  121.7 1.0 multiply_cosine_fusion
  122.7 39.9 %all-gather.6.cloned.1.call-done = bf16[1024,4608]{1,0:T(8,128)(2,1)} async-done(((bf16[1024,1152]{1,0:T(8,128)(2,1)}), bf16[1024,4608]{1,0:T(8,128)(2,1)}) %all-gather.6.cloned.1.call-update) | async-done | bytes 9437200 | tf_op jit(solution)/shard_map/all_gather | solution.py:101
  162.6 9.1 %fusion.38 = f32[1024,512]{0,1:T(8,128)S(1)} fusion(bf16[1024,4608]{1,0:T(8,128)(2,1)} %all-gather.6.cloned.1.call-done, bf16[4608,512]{1,0:T(8,128)(2,1)} %all-gather.12.cloned.1.call-done), kind=kOutput, calls=%fused_computation.88 | convolution fusion | flops 4831838208 | bytes 16252928 | tf_op jit(solution)/shard_map/dot_general | solution.py:107
  172.7 9.2 %concatenate.11 = bf16[1216,4608]{1,0:T(8,128)(2,1)} pad(bf16[1024,4608]{1,0:T(8,128)(2,1)} %all-gather.6.cloned.1.call-done, bf16[]{:T(256)} %constant.127.clone.1), padding=0_192x0_0 | pad | bytes 20643842 | tf_op jit(solution)/shard_map/concatenate | solution.py:70
  181.8 35.0 %all-gather.10.cloned.1.call-done = bf16[8,4608,32]{1,2,0:T(8,128)(2,1)} async-done(((bf16[1,4608,32]{1,2,0:T(8,128)(2,1)}), bf16[8,4608,32]{1,2,0:T(8,128)(2,1)}) %all-gather.10.cloned.1.call-update) | async-done | bytes 2359312 | tf_op jit(solution)/shard_map/all_gather | solution.py:123
  216.9 91.5 %while.14 = (s32[]{:T(128)}, f32[1216,32]{0,1:T(8,128)S(1)}, s32[10]{0:T(128)S(1)}, bf16[1216,4608]{1,0:T(8,128)(2,1)}, s32[10]{0:T(128)S(1)}, /*index=5*/bf16[8...) while((s32[]{:T(128)}, f32[1216,32]{0,1:T(8,128)S(1)}, ...), condition=%wide.region_3.5_spmd.clone, body=%wide.region_2.4_spmd.clone.sunk | while | flops 56635784 | bytes 2165981 | solution.py:83
  223.2 2.3 fusion.53
  232.3 2.2 fusion.53
  241.4 2.2 fusion.53
  250.6 2.2 fusion.53
  259.7 2.2 fusion.53
  268.9 2.2 fusion.53
  278.0 2.2 fusion.53
  287.2 2.2 fusion.53
  296.3 2.2 fusion.53
  305.4 2.4 fusion.53
  308.4 6.8 %scatter_custom_fusion = bf16[2304,512]{1,0:T(8,128)(2,1)} fusion(s32[1024]{0:T(1024)S(1)} %get-tuple-element.188, bf16[1024,512]{1,0:T(8,128)(2,1)S(1)} %copy.27, bf16[]{:T(256)} %constant.127.clone.1), kind=kCustom, calls=%fused_computation.20 | custom fusion | bytes 2359298 | tf_op jit(solution)/shard_map/scatter | solution.py:136
  315.2 9.0 %fusion.39 = f32[1024,512]{1,0:T(8,128)S(1)} fusion(bf16[1024,4608]{1,0:T(8,128)(2,1)} %all-gather.6.cloned.1.call-done, bf16[4608,512]{1,0:T(8,128)(2,1)} %all-gather.14.cloned.1.call-done), kind=kOutput, calls=%fused_computation.89 | convolution fusion | flops 4831838208 | bytes 16252928 | tf_op jit(solution)/shard_map/dot_general | solution.py:112
  324.7 6.8 %scatter_custom_fusion.1 = bf16[2304,512]{1,0:T(8,128)(2,1)} fusion(s32[1024]{0:T(1024)S(1)} %get-tuple-element.188, bf16[1024,512]{1,0:T(8,128)(2,1)S(1)} %fusion.13, bf16[]{:T(256)} %constant.127.clone.1), kind=kCustom, calls=%fused_computation.18 | custom fusion | bytes 2359298 | tf_op jit(solution)/shard_map/scatter | solution.py:142
  331.6 104.1 %all-gather.8.cloned.1.call-done = bf16[4608,1024]{1,0:T(8,128)(2,1)} async-done(((bf16[576,1024]{1,0:T(8,128)(2,1)}), bf16[4608,1024]{1,0:T(8,128)(2,1)}) %all-gather.8.cloned.1.call-update) | async-done | bytes 9437200 | tf_op jit(solution)/shard_map/all_gather | solution.py:104
  435.6 14.6 %fusion.37 = f32[1024,1024]{0,1:T(8,128)S(1)} fusion(bf16[1024,4608]{1,0:T(8,128)(2,1)} %all-gather.6.cloned.1.call-done, bf16[4608,1024]{1,0:T(8,128)(2,1)} %all-gather.8.cloned.1.call-done), kind=kOutput, calls=%fused_computation.87 | convolution fusion | flops 9663676416 | bytes 23068672 | tf_op jit(solution)/shard_map/dot_general | solution.py:102
  450.2 0.8 bitcast_add_fusion
  451.0 0.8 subtract_convert_fusion
  452.0 2.6 copy.26
  (99 shorter events, 36.7 us)
Async XLA Ops:
  7.2 11.1 %copy-start = (s32[8]{0:T(128)S(1)}, s32[8]{0:T(128)}, u32[]{:S(2)}) copy-start(s32[8]{0:T(128)} %param.24) | copy-start | bytes 100
  7.2 1.6 copy-start.3
  7.2 115.5 %all-gather.12.cloned.1.call-start = ((), (), s32[]{:S(2)}) async-start(), calls=%async_computation.3 | async-start | bytes 5308416 | tf_op jit(solution)/shard_map/all_gather | solution.py:109
  7.9 9.9 %copy-start.7 = (s32[1,10]{1,0:T(1,128)S(1)}, s32[1,10]{1,0:T(1,128)}, u32[]{:S(2)}) copy-start(s32[1,10]{1,0:T(1,128)} %param.22) | copy-start | bytes 124
  7.9 10.3 %copy-start.6 = (s32[1,10]{1,0:T(1,128)S(1)}, s32[1,10]{1,0:T(1,128)}, u32[]{:S(2)}) copy-start(s32[1,10]{1,0:T(1,128)} %param.23) | copy-start | bytes 124
  7.9 11.0 %copy-start.5 = (bf16[1,16,512]{2,1,0:T(8,128)(2,1)S(1)}, bf16[1,16,512]{2,1,0:T(8,128)(2,1)}, u32[]{:S(2)}) copy-start(bf16[1,16,512]{2,1,0:T(8,128)(2,1)} %param.21) | copy-start | bytes 49156
  8.0 44.6 %copy-start.2 = (s32[1,18]{1,0:T(1,128)S(1)}, s32[1,18]{1,0:T(1,128)}, u32[]{:S(2)}) copy-start(s32[1,18]{1,0:T(1,128)} %param.25) | copy-start | bytes 220
  8.0 45.4 %copy-start.4 = (bf16[1,16,1024]{2,1,0:T(8,128)(2,1)S(1)}, bf16[1,16,1024]{2,1,0:T(8,128)(2,1)}, u32[]{:S(2)}) copy-start(bf16[1,16,1024]{2,1,0:T(8,128)(2,1)} %param.20) | copy-start | bytes 98308
  8.0 154.6 %all-gather.6.cloned.1.call-start = ((), (), s32[]{:S(2)}) async-start(), calls=%async_computation | async-start | bytes 11796480 | tf_op jit(solution)/shard_map/all_gather | solution.py:101
  8.7 208.2 %all-gather.10.cloned.1.call-start = ((), (), s32[]{:S(2)}) async-start(), calls=%async_computation.2 | async-start | bytes 2654208 | tf_op jit(solution)/shard_map/all_gather | solution.py:123
  16.7 298.6 %all-gather.14.cloned.1.call-start = ((), (), s32[]{:S(2)}) async-start(), calls=%async_computation.4 | async-start | bytes 5308416 | tf_op jit(solution)/shard_map/all_gather | solution.py:114
  17.3 418.4 %all-gather.8.cloned.1.call-start = ((), (), s32[]{:S(2)}) async-start(), calls=%async_computation.1 | async-start | bytes 10616832 | tf_op jit(solution)/shard_map/all_gather | solution.py:104
  451.8 2.8 copy-start.1
Sparse Core Ops, SparseCore 0:
  10.2 88.2 all-gather.11
  100.1 62.4 all-gather.5
  164.8 52.0 all-gather.9
  218.9 78.4 all-gather.13
  299.4 136.1 all-gather.7
where the time goes:
time: 463 us; the launch traced here: 461 us
  waiting for transfers between devices  181 us (39%)
  blocking collectives  71.2 us (15%)
  matrix products  56.3 us (12%)
  local copies, waits for them, and re-layouts  52.7 us (11%)
  other arithmetic  45.8 us (10%)
  loops' own time  39.3 us (8%)
  between operations  14 us (3%)
    all_gather x1, waiting for transfers between devices, shards(): lax.all_gather(w_query, 'col', axis=0, tiled=True)  104 us
    all_gather x1, waiting for transfers between devices, shards(): full_rows = lax.all_gather(hidden, 'row', axis=1, tiled=True)  39.9 us
    another operation x1, loops' own time, project_down(): result = lax.fori_loop(0, starts.shape[0], one_request, result)  39.3 us
    all_gather x1, waiting for transfers between devices, shards(): down_all = lax.all_gather(rows_all, 'col', axis=0, tiled=True)  35 us
    all_gather x1, blocking collectives, shards(): lax.all_gather(adapter_up_query, 'col', axis=0, tiled=True)  31.8 us
    all_gather x1, blocking collectives, shards(): lax.all_gather(adapter_up_value, 'col', axis=0, tiled=True)  31.5 us
    select_n x1, other arithmetic, shards(): key_cache = jnp.zeros((pages * PAGE, key_width), jnp.bfloat16).at[target]...  23.9 us
    dot_general x10, matrix products, one_request(): partial_sum = jnp.dot(window, factor, preferred_element_type=jnp.float32)  22.4 us
  transfers between devices with their start and end apart: 5, of which 3 were waited for; matrix products, arithmetic and copies ran while one was open for 29% of the time, Pallas kernels for 0%

commit v1 on v0

v1 whole, which is shorter than its diff:
```python
import functools
import math

import jax
import jax.numpy as jnp
from jax import lax
from jax.experimental import pallas as pl
from jax.experimental.pallas import tpu as pltpu
from jax.sharding import PartitionSpec as P

HEAD = 128
PAGE = 128
TOK = 1024
CHUNKS = 8
AHEAD = 3
TILE = 256
MESH = pl.DeviceIdType.MESH
BF16 = jnp.bfloat16
F32 = jnp.float32


def project(nc, nr, h2, w, raw, dn_in, up_in, pos, slot, freq, q_out, kv_out,
            wbuf, hid, acc, sendb, precv, dn, up, lr, sq, sv, cosb, sinb,
            local, wsend, wrecv, hsend, hrecv, csend, xsend, xrecv,
            psend, pget, dsend, drecv, usend, urecv, lsend, lrecv):
    nb = nc // 2
    per = nb // nr
    kb, cw = wbuf.shape[2], wbuf.shape[3]
    rank = up_in.shape[0]
    kw = kv_out.shape[1] // 2
    c = lax.axis_index("col")
    r = lax.axis_index("row")
    p = c // 2
    x = c % 2
    other = 1 - x
    mate = c + 1 - 2 * x
    twin = r + 1 - 2 * (r % 2)

    def remote(src, dst, ssem, rsem, **where):
        return pltpu.make_async_remote_copy(
            src_ref=src, dst_ref=dst, send_sem=ssem, recv_sem=rsem,
            device_id=where, device_id_type=MESH)

    loads = [
        pltpu.make_async_copy(w, wbuf.at[p], local.at[0]),
        pltpu.make_async_copy(h2.at[x], hid.at[r, x], local.at[1]),
        pltpu.make_async_copy(dn_in, dn.at[c], local.at[2]),
        pltpu.make_async_copy(up_in, up.at[c], local.at[3]),
    ]
    for one in loads:
        one.start()

    barrier = pltpu.get_barrier_semaphore()

    @pl.loop(1, nc)
    def _(m):
        pl.semaphore_signal(barrier, inc=1, device_id={"col": (c + m) % nc}, device_id_type=MESH)

    @pl.loop(1, nr)
    def _(m):
        pl.semaphore_signal(barrier, inc=1, device_id={"row": (r + m) % nr}, device_id_type=MESH)

    pl.semaphore_wait(barrier, nc + nr - 2)
    for one in loads:
        one.wait()

    def weight(b, j, side):
        to = jnp.clip(c + 2 if side else c - 2, 0, nc - 1)
        return remote(wbuf.at[b, j], wbuf.at[b, j], wsend.at[side, b, j], wrecv.at[b, j], col=to)

    def send_own(j):
        @pl.when(p + 1 < nb)
        def _():
            weight(p, j, 1).start()

        @pl.when(p > 0)
        def _():
            weight(p, j, 0).start()

    def service(j):
        @pl.loop(1, nb)
        def _(d):
            @pl.when(p - d >= 0)
            def _():
                weight(p - d, j, 1).wait_recv()

                @pl.when(p + 1 < nb)
                def _():
                    weight(p - d, j, 1).start()

            @pl.when(p + d < nb)
            def _():
                weight(p + d, j, 0).wait_recv()

                @pl.when(p > 0)
                def _():
                    weight(p + d, j, 0).start()

        if j + AHEAD < CHUNKS:
            send_own(j + AHEAD)

    def to_mate():
        return remote(h2.at[other], hid.at[r, x], xsend, xrecv, col=mate)

    def from_mate():
        return remote(h2.at[other], hid.at[r, other], xsend, xrecv, col=mate)

    def to_peer(t, m):
        return remote(hid.at[r, t], hid.at[r, t], hsend.at[t, m], hrecv.at[r, t], row=(r + 2 * m) % nr)

    def to_twin(o, t):
        return remote(hid.at[o, t], hid.at[o, t], csend.at[o, t], hrecv.at[o, t], row=twin)

    def arrived(o, t):
        remote(hid.at[o, t], hid.at[o, t], csend.at[o, t], hrecv.at[o, t], row=twin).wait_recv()

    def spread_hidden(t):
        for m in range(1, nr // 2):
            to_peer(t, m).start()
        to_twin(r, t).start()

    def pass_hidden(t):
        for m in range(1, nr // 2):
            o = (r + 2 * m) % nr
            arrived(o, t)
            to_twin(o, t).start()

    def settle_hidden(t):
        for m in range(nr // 2):
            arrived((twin + 2 * m) % nr, t)

    def down_copy(owner, m):
        return remote(dn.at[owner], dn.at[owner], dsend.at[m], drecv.at[owner], col=(c + m) % nc)

    def up_copy(owner, m):
        return remote(up.at[owner], up.at[owner], usend.at[m], urecv.at[owner], col=(c + m) % nc)

    def low_copy(owner, m):
        return remote(lr.at[owner], lr.at[owner], lsend.at[m], lrecv.at[owner], row=(r + m) % nr)

    def lowrank_start():
        @pl.loop(1, nc)
        def _(m):
            down_copy((c + m) % nc, m).wait_recv()

        everything = lax.dot_general(
            dn[...].reshape(nc * 2 * rank, raw.shape[1]), raw[...],
            (((1,), (1,)), ((), ())), preferred_element_type=F32)
        which = slot[...]
        mine = jnp.zeros((2 * rank, TOK), F32)
        for a in range(nc):
            mine = mine + jnp.where(which == a, everything[a * 2 * rank:(a + 1) * 2 * rank], 0.0)
        lr[r] = mine

        @pl.loop(1, nr)
        def _(m):
            low_copy(r, m).start()

    def lowrank_end():
        @pl.loop(1, nr)
        def _(m):
            low_copy((r + m) % nr, m).wait_recv()

        @pl.loop(1, nc)
        def _(m):
            up_copy((c + m) % nc, m).wait_recv()

        total = lr[0]
        for o in range(1, nr):
            total = total + lr[o]
        which = slot[...]
        for ref, part in ((sq, total[:rank]), (sv, total[rank:])):
            tall = jnp.concatenate([jnp.where(which == a, part, 0.0) for a in range(nc)], axis=0)
            ref[...] = tall.T.astype(BF16)

    def tables():
        @pl.loop(0, TOK // TILE)
        def _(i):
            rows = pl.ds(pl.multiple_of(i * TILE, TILE), TILE)
            angle = pos[rows, :] * freq[...]
            sign = jnp.where(lax.broadcasted_iota(jnp.int32, (TILE, HEAD), 1) < HEAD // 2, -1.0, 1.0)
            cosb[rows, :] = jnp.cos(angle)
            sinb[rows, :] = jnp.sin(angle) * sign

    def product(j, half, rows):
        total = None
        for o in range(nr):
            factor = wbuf[o * per:(o + 1) * per, j].reshape(per * kb, cw)
            term = jnp.dot(hid[o, half, rows, :], factor, preferred_element_type=F32)
            total = term if total is None else total + term
        return total

    def part_copy(j):
        return remote(sendb.at[j], precv.at[j], psend.at[j], pget.at[j], col=mate)

    def compute(j):
        @pl.loop(0, TOK // TILE)
        def _(i):
            rows = pl.ds(pl.multiple_of(i * TILE, TILE), TILE)
            sendb[j, rows, :] = product(j, other, rows).astype(BF16)

        part_copy(j).start()

        @pl.loop(0, TOK // TILE)
        def _(i):
            rows = pl.ds(pl.multiple_of(i * TILE, TILE), TILE)
            acc[j, rows, :] = product(j, x, rows)

    def combine(j):
        part_copy(j).wait_recv()

        @pl.loop(0, TOK // TILE)
        def _(i):
            rows = pl.ds(pl.multiple_of(i * TILE, TILE), TILE)
            v = acc[j, rows, :] + precv[j, rows, :].astype(F32)
            if j >= 2:
                at = (j - 2) * cw
                factor = up[:, :, at:at + cw].reshape(nc * rank, cw)
                lowered = sq if j < 6 else sv
                v = v + jnp.dot(lowered[rows, :], factor, preferred_element_type=F32)
            if j < 6:
                heads = []
                for k in range(cw // HEAD):
                    one = v[:, k * HEAD:(k + 1) * HEAD]
                    heads.append(one * cosb[rows, :] + pltpu.roll(one, HEAD // 2, 1) * sinb[rows, :])
                v = heads[0] if len(heads) == 1 else jnp.concatenate(heads, axis=1)
            v = v.astype(BF16)
            if j < 2:
                kv_out[rows, j * cw:(j + 1) * cw] = v
            elif j < 6:
                q_out[rows, (j - 2) * cw:(j - 1) * cw] = v
            else:
                kv_out[rows, kw + (j - 6) * cw:kw + (j - 5) * cw] = v

    to_mate().start()
    spread_hidden(x)
    send_own(0)

    @pl.loop(1, nc)
    def _(m):
        down_copy(c, m).start()
        up_copy(c, m).start()

    for j in range(1, AHEAD):
        send_own(j)
    tables()
    service(0)
    from_mate().wait_recv()
    spread_hidden(other)
    pass_hidden(x)
    service(1)
    lowrank_start()
    service(2)
    pass_hidden(other)
    settle_hidden(x)
    settle_hidden(other)
    compute(0)
    service(3)
    compute(1)
    compute(2)
    lowrank_end()
    service(4)
    combine(0)
    compute(3)
    compute(4)
    combine(1)
    for j in range(5, CHUNKS):
        service(j)
        compute(j)
        combine(j - 3)
    for j in range(CHUNKS - 3, CHUNKS):
        combine(j)

    @pl.loop(0, CHUNKS)
    def _(j):
        @pl.loop(0, nb)
        def _(b):
            @pl.when((b <= p) & (p + 1 < nb))
            def _():
                weight(b, j, 1).wait_send()

            @pl.when((b >= p) & (p > 0))
            def _():
                weight(b, j, 0).wait_send()

        part_copy(j).wait_send()

    to_mate().wait_send()
    for t in range(2):
        for m in range(1, nr // 2):
            to_peer(t, m).wait_send()
        for m in range(nr // 2):
            to_twin((r + 2 * m) % nr, t).wait_send()

    @pl.loop(1, nc)
    def _(m):
        down_copy(c, m).wait_send()
        up_copy(c, m).wait_send()

    @pl.loop(1, nr)
    def _(m):
        low_copy(r, m).wait_send()


def paging(table, first, count, kv, key, value):
    n = pl.program_id(0)
    window = PAGE + 16
    kw = key.shape[2]
    base = pl.multiple_of(jnp.minimum(first[n] // 16 * 16, TOK - window), 16)
    row = lax.broadcasted_iota(jnp.int32, (PAGE, window), 0)
    column = lax.broadcasted_iota(jnp.int32, (PAGE, window), 1)
    pick = ((column == row + (first[n] - base)) & (row < count[n])).astype(F32).astype(BF16)
    rows = jnp.dot(pick, kv[pl.ds(base, window), :], preferred_element_type=F32).astype(BF16)
    key[0] = rows[:, :kw]
    value[0] = rows[:, kw:]


def shards(nc, nr, hidden, w_query, w_key, w_value, adapter_down, adapter_up_query,
           adapter_up_value, lengths, request_adapter, adapter_slot, page_table):
    kb = w_query.shape[0]
    qw, kw = w_query.shape[1], w_key.shape[1]
    width = qw + 2 * kw
    cw = width // CHUNKS
    hw = hidden.shape[1]
    rank = adapter_up_query.shape[1]
    pages = page_table.shape[1]
    nb = nc // 2

    lengths, page_row = lengths[0], page_table[0]
    starts = jnp.cumsum(lengths) - lengths
    token = jnp.arange(TOK, dtype=jnp.int32)
    after = token[:, None] >= starts[None, :]
    within = after & (token[:, None] < (starts + lengths)[None, :])
    position = token - jnp.max(jnp.where(after, starts[None, :], 0), axis=1)
    adapters = jnp.arange(nc, dtype=jnp.int32)
    chosen_request = jnp.sum(
        jnp.where(request_adapter[0][:, None] == adapters[None, :], adapter_slot[None, :], 0), axis=1)
    chosen = jnp.sum(jnp.where(within, chosen_request[None, :], 0), axis=1)
    frequency = jnp.exp(jnp.arange(HEAD // 2, dtype=F32) * (-2.0 * math.log(10000.0) / HEAD))
    frequency = jnp.concatenate([frequency, frequency])[None, :]

    pages_each = (lengths + PAGE - 1) // PAGE
    page_start = jnp.cumsum(pages_each) - pages_each
    number = jnp.arange(pages, dtype=jnp.int32)
    started = number[:, None] >= page_start[None, :]
    owner = jnp.sum(started.astype(jnp.int32), axis=1) - 1
    mine = owner[:, None] == jnp.arange(lengths.shape[0], dtype=jnp.int32)[None, :]
    offset = (number - jnp.sum(jnp.where(mine, page_start[None, :], 0), axis=1)) * PAGE
    first = jnp.minimum(jnp.sum(jnp.where(mine, starts[None, :], 0), axis=1) + offset, TOK - 1)
    count = jnp.clip(jnp.sum(jnp.where(mine, lengths[None, :], 0), axis=1) - offset, 0, PAGE)

    w = jnp.concatenate([w_key, w_query, w_value], axis=1)
    w = w.reshape(kb, CHUNKS, cw).transpose(1, 0, 2)
    h2 = hidden.reshape(TOK, hw // (2 * kb), 2, kb).transpose(2, 0, 1, 3).reshape(2, TOK, hw // 2)
    down = adapter_down[0].T
    up = jnp.concatenate([adapter_up_query[0], adapter_up_value[0]], axis=1)

    hbm = pl.BlockSpec(memory_space=pl.ANY)
    vmem = pl.BlockSpec(memory_space=pltpu.VMEM)
    dma = pltpu.SemaphoreType.DMA
    query, kv = pl.pallas_call(
        functools.partial(project, nc, nr),
        out_shape=(jax.ShapeDtypeStruct((TOK, qw), BF16), jax.ShapeDtypeStruct((TOK, 2 * kw), BF16)),
        in_specs=[hbm, hbm, vmem, hbm, hbm, vmem, vmem, vmem],
        out_specs=(vmem, vmem),
        scratch_shapes=[
            pltpu.VMEM((nb, CHUNKS, kb, cw), BF16),
            pltpu.VMEM((nr, 2, TOK, hw // 2), BF16),
            pltpu.VMEM((CHUNKS, TOK, cw), F32),
            pltpu.VMEM((CHUNKS, TOK, cw), BF16),
            pltpu.VMEM((CHUNKS, TOK, cw), BF16),
            pltpu.VMEM((nc, 2 * rank, hw), BF16),
            pltpu.VMEM((nc, rank, qw + kw), BF16),
            pltpu.VMEM((nr, 2 * rank, TOK), F32),
            pltpu.VMEM((TOK, nc * rank), BF16),
            pltpu.VMEM((TOK, nc * rank), BF16),
            pltpu.VMEM((TOK, HEAD), F32),
            pltpu.VMEM((TOK, HEAD), F32),
            dma((4,)),
            dma((2, nb, CHUNKS)),
            dma((nb, CHUNKS)),
            dma((2, nr)),
            dma((nr, 2)),
            dma((nr, 2)),
            dma,
            dma,
            dma((CHUNKS,)),
            dma((CHUNKS,)),
            dma((nc,)),
            dma((nc,)),
            dma((nc,)),
            dma((nc,)),
            dma((nr,)),
            dma((nr,)),
        ],
        compiler_params=pltpu.CompilerParams(
            collective_id=0, has_side_effects=True, vmem_limit_bytes=60 * 1024 * 1024),
        name="project",
    )(h2, w, hidden, down, up, position.astype(F32)[:, None], chosen[None, :], frequency)

    key_cache, value_cache = pl.pallas_call(
        paging,
        out_shape=(jax.ShapeDtypeStruct((pages, PAGE, kw), BF16),) * 2,
        grid_spec=pltpu.PrefetchScalarGridSpec(
            num_scalar_prefetch=3,
            grid=(pages,),
            in_specs=[pl.BlockSpec((TOK, 2 * kw), lambda n, table, first, count: (0, 0))],
            out_specs=[pl.BlockSpec((1, PAGE, kw), lambda n, table, first, count: (table[n], 0, 0))] * 2,
        ),
        compiler_params=pltpu.CompilerParams(vmem_limit_bytes=32 * 1024 * 1024),
        name="paging",
    )(page_row, first, count, kv)
    return (query, key_cache, value_cache)


def solution(mesh):
    return jax.shard_map(
        functools.partial(shards, mesh.shape["col"], mesh.shape["row"]),
        mesh=mesh,
        in_specs=(
            P("col", "row"),
            P("col", "row"),
            P("col", "row"),
            P("col", "row"),
            P("col", "row", None),
            P("col", None, "row"),
            P("col", None, "row"),
            P("col", None),
            P("col", None),
            P(),
            P("col", None),
        ),
        out_specs=(P("col", "row"), P("col", None, "row"), P("col", None, "row")),
        check_vma=False,
    )
```

time: 463 us -> 234 us (0.51)
  Pallas kernels: 0 us -> 214 us
  waiting for transfers between devices: 181 us -> 0 us
  blocking collectives: 71.2 us -> 0 us
  matrix products: 56.3 us -> 0 us
  local copies, waits for them, and re-layouts: 52.7 us -> 10.1 us
  loops' own time: 39.3 us -> 0 us
  other arithmetic: 45.8 us -> 8.43 us
  between operations: 14 us -> 0.7 us
    pallas_call x0 -> x2, Pallas kernels: none -> 214 us  [the longest x1 206 us: shards(): pl.pallas_call(functools.partial(project, nc, nr), out_shape=(jax.ShapeDt...]
    all_gather x5 -> x0, waiting for transfers between devices: 179 us -> none  [the longest x1 104 us: shards(): lax.all_gather(w_query, 'col', axis=0, tiled=True)]
    all_gather x3 -> x0, blocking collectives: 71.2 us -> none  [the longest x1 31.8 us: shards(): lax.all_gather(adapter_up_query, 'col', axis=0, tiled=True)]
    dot_general x15 -> x0, matrix products: 56.3 us -> none  [the longest x10 22.4 us: one_request(): partial_sum = jnp.dot(window, factor, preferred_element_type=jnp.float32)]
    another operation x1 -> x0, loops' own time: 39.3 us -> none  [project_down(): result = lax.fori_loop(0, starts.shape[0], one_request, result)]
    select_n x4 -> x1, other arithmetic: 30.1 us -> 0.66 us  [shards(): pages_each = (lengths + PAGE - 1) // PAGE]
    dynamic_slice x30 -> x0, local copies, waits for them, and re-layouts: 17.6 us -> none  [the longest x10 5.89 us: one_request(): inside = (inner_rows < lengths[number]).astype(jnp.float32)[:, None]]
    scatter x2 -> x0, local copies, waits for them, and re-layouts: 13.6 us -> none  [the longest x1 6.82 us: shards(): key_cache = jnp.zeros((pages * PAGE, key_width), jnp.bfloat16).at[target]...]
  transfers between devices with their start and end apart: 5 -> 0, of which waited for: 3 -> 0; matrix products, arithmetic and copies ran while one was open for 29% -> 0% of each run, Pallas kernels for 0% -> 0%
where the time goes in v1:
time: 234 us
  Pallas kernels  214 us (91%)
  local copies, waits for them, and re-layouts  10.1 us (4%)
  other arithmetic  8.43 us (4%)
    pallas_call x1, Pallas kernels, shards(): pl.pallas_call(functools.partial(project, nc, nr), out_shape=(jax.ShapeDt...  206 us
    pallas_call x1, Pallas kernels, shards(): pl.pallas_call(paging, out_shape=(jax.ShapeDtypeStruct((pages, PAGE, kw),...  8.76 us
    unnamed x10, local copies, waits for them, and re-layouts  5.75 us

profile of v1, /device:TPU:0, one launch (start us, length us, event | category | flops | bytes accessed | tf_op | source)
XLA Modules:
  0.0 233.6 jit_solution(8926047415798576331)
XLA Ops:
  0.6 0.0 copy-start.3
  0.6 0.9 reduce-window.6
  1.6 0.8 select_reduce_fusion.5
  2.3 0.6 maximum_bitcast_fusion.freq
  2.9 0.7 and_select_fusion
  3.6 0.2 reduce-window_1_clone.1
  3.8 0.1 convert_reduce_fusion
  3.9 0.7 select_reduce_fusion.2
  4.6 0.7 select_reduce_fusion
  5.3 1.4 pad_maximum_fusion.1.up_in
  6.7 0.2 copy.25
  7.0 0.8 convert_element_type.13.pos
  7.8 0.0 copy-done.3
  7.8 1.5 pad_maximum_fusion
  9.3 1.6 copy.28
  10.9 2.8 %copy.22 = bf16[1024,1152]{0,1:T(8,128)(2,1)S(1)} copy(bf16[1024,1152]{1,0:T(8,128)(2,1)} %raw.1) | data formatting | bytes 4718592 | tf_op args[0]
  13.7 2.6 %copy.23 = bf16[1024,1,2,576]{3,0,2,1:T(8,128)(2,1)} copy(bf16[1024,1,2,576]{0,3,2,1:T(8,128)(2,1)S(1)} %bitcast.36) | data formatting | bytes 4718592 | tf_op jit(solution)/shard_map/reshape | solution.py:354
  16.3 0.0 copy-start.1
  16.3 205.6 %project.1 = (bf16[1024,1024]{1,0:T(8,128)(2,1)}, bf16[1024,1024]{1,0:T(8,128)(2,1)}) custom-call(bf16[2,1024,576]{2,1,0:T(8,128)(2,1)} %bitcast.34, bf16[8,576,256]{2,1,0:T(8,128)(2,1)} %bitcast.37, bf16[1024,1152]{1,0:T(8,128)(2,1)} %raw.1, bf16[32,1152]{1,0:T(8,128)(2,1)} %bitcast.38, bf16[16,1536]{1,0:T(8,128)(2,1)} %pad_maximum_fusion.1.up_in, ...), custom_call_target="tpu_custom_call" | custom-call | tf_op jit(solution)/shard_map/project/pallas_call | solution.py:361
  221.9 0.0 copy-done.1
  222.0 0.0 copy-start
  222.0 1.6 copy-done
  223.5 0.0 copy-start.2
  223.6 8.8 %paging.1 = (bf16[18,128,512]{2,1,0:T(8,128)(2,1)}, bf16[18,128,512]{2,1,0:T(8,128)(2,1)}) custom-call(s32[18]{0:T(128)S(1)} %bitcast.33, s32[18]{0:T(128)S(1)} %get-tuple-element.17.first, s32[18]{0:T(128)S(1)} %get-tuple-element.16.count, bf16[1024,1024]{1,0:T(8,128)(2,1)S(1)} %copy-done), custom_call_target="tpu_custom_call" | custom-call | tf_op jit(solution)/shard_map/paging/pallas_call | solution.py:401
  232.3 0.0 copy-done.2
  232.3 1.3 copy.30
  (5 shorter events, 0.0 us)
Async XLA Ops:
  0.6 7.2 %copy-start.3 = (bf16[576,1024]{1,0:T(8,128)(2,1)S(1)}, bf16[576,1024]{1,0:T(8,128)(2,1)}, u32[]{:S(2)}) copy-start(bf16[576,1024]{1,0:T(8,128)(2,1)} %param.12) | copy-start | bytes 3538948
  16.3 205.6 %copy-start.1 = (s32[1,18]{1,0:T(1,128)S(1)}, s32[1,18]{1,0:T(1,128)}, u32[]{:S(2)}) copy-start(s32[1,18]{1,0:T(1,128)} %param.21) | copy-start | bytes 220
  222.0 1.6 copy-start
  223.5 8.8 %copy-start.2 = (bf16[1024,1024]{1,0:T(8,128)(2,1)S(1)}, bf16[1024,1024]{1,0:T(8,128)(2,1)}, u32[]{:S(2)}) copy-start(bf16[1024,1024]{1,0:T(8,128)(2,1)} %get-tuple-element.23) | copy-start | bytes 6291460

commit v2 on v1

--- a/solution.py
+++ b/solution.py
@@ -3,6 +3,7 @@
 
 import jax
 import jax.numpy as jnp
+import numpy as np
 from jax import lax
 from jax.experimental import pallas as pl
 from jax.experimental.pallas import tpu as pltpu
@@ -14,19 +15,22 @@
 CHUNKS = 8
 AHEAD = 3
 TILE = 256
+HALF = 512
 MESH = pl.DeviceIdType.MESH
 BF16 = jnp.bfloat16
 F32 = jnp.float32
 
 
-def project(nc, nr, h2, w, raw, dn_in, up_in, pos, slot, freq, q_out, kv_out,
-            wbuf, hid, acc, sendb, precv, dn, up, lr, sq, sv, cosb, sinb,
-            local, wsend, wrecv, hsend, hrecv, csend, xsend, xrecv,
-            psend, pget, dsend, drecv, usend, urecv, lsend, lrecv):
+def project(nc, nr, raw, w_query, w_key, w_value, dn_in, upq_in, upv_in, freq,
+            lengths, request_adapter, adapter_slot, q_out, kv_out,
+            wbuf, h2, hid, acc, sendb, precv, dn, up, lr, sq, sv, cosb, sinb,
+            wload, local, wsend, wrecv, hsend, hrecv, csend, xsend, xrecv,
+            psend, pget, dsend, dmate, drecv, usend, umate, urecv, lsend, lrecv):
     nb = nc // 2
     per = nb // nr
     kb, cw = wbuf.shape[2], wbuf.shape[3]
-    rank = up_in.shape[0]
+    rank = upq_in.shape[1]
+    qw = upq_in.shape[2]
     kw = kv_out.shape[1] // 2
     c = lax.axis_index("col")
     r = lax.axis_index("row")
@@ -42,13 +46,28 @@
             device_id=where, device_id_type=MESH)
 
     loads = [
-        pltpu.make_async_copy(w, wbuf.at[p], local.at[0]),
-        pltpu.make_async_copy(h2.at[x], hid.at[r, x], local.at[1]),
-        pltpu.make_async_copy(dn_in, dn.at[c], local.at[2]),
-        pltpu.make_async_copy(up_in, up.at[c], local.at[3]),
+        pltpu.make_async_copy(dn_in, dn.at[c], local.at[0]),
+        pltpu.make_async_copy(upq_in.at[0], up.at[c, :, :qw], local.at[1]),
+        pltpu.make_async_copy(upv_in.at[0], up.at[c, :, qw:], local.at[2]),
     ]
+    for j in range(CHUNKS):
+        if j < 2:
+            src, at = w_key, j * cw
+        elif j < 6:
+            src, at = w_query, (j - 2) * cw
+        else:
+            src, at = w_value, (j - 6) * cw
+        loads.append(pltpu.make_async_copy(src.at[:, at:at + cw], wbuf.at[p, j], wload.at[j]))
     for one in loads:
         one.start()
+
+    @pl.loop(0, TOK // TILE)
+    def _(i):
+        rows = pl.ds(pl.multiple_of(i * TILE, TILE), TILE)
+        for s in range(2):
+            parts = [raw[rows, (2 * g + s) * kb:(2 * g + s + 1) * kb] for g in range(per)]
+            h2[s, rows, :] = parts[0] if per == 1 else jnp.concatenate(parts, axis=1)
+        hid[r, x, rows, :] = h2[x, rows, :]
 
     barrier = pltpu.get_barrier_semaphore()
 
@@ -129,24 +148,83 @@
         for m in range(nr // 2):
             arrived((twin + 2 * m) % nr, t)
 
-    def down_copy(owner, m):
-        return remote(dn.at[owner], dn.at[owner], dsend.at[m], drecv.at[owner], col=(c + m) % nc)
-
-    def up_copy(owner, m):
-        return remote(up.at[owner], up.at[owner], usend.at[m], urecv.at[owner], col=(c + m) % nc)
+    def factors(b, side):
+        owner = 2 * b + x
+        to = jnp.clip(c + 2 if side else c - 2, 0, nc - 1)
+        return (remote(dn.at[owner], dn.at[owner], dsend.at[side, b], drecv.at[owner], col=to),
+                remote(up.at[owner], up.at[owner], usend.at[side, b], urecv.at[owner], col=to))
+
+    def factors_mate(b, parity):
+        owner = 2 * b + parity
+        return (remote(dn.at[owner], dn.at[owner], dmate.at[b], drecv.at[owner], col=mate),
+                remote(up.at[owner], up.at[owner], umate.at[b], urecv.at[owner], col=mate))
+
+    def start(pair):
+        for one in pair:
+            one.start()
+
+    def send_factors():
+        @pl.when(p + 1 < nb)
+        def _():
+            start(factors(p, 1))
+
+        @pl.when(p > 0)
+        def _():
+            start(factors(p, 0))
+
+        start(factors_mate(p, x))
+
+    def service_factors():
+        @pl.loop(1, nb)
+        def _(d):
+            @pl.when(p - d >= 0)
+            def _():
+                for one in factors(p - d, 1):
+                    one.wait_recv()
+
+                @pl.when(p + 1 < nb)
+                def _():
+                    start(factors(p - d, 1))
+
+                start(factors_mate(p - d, x))
+
+            @pl.when(p + d < nb)
+            def _():
+                for one in factors(p + d, 0):
+                    one.wait_recv()
+
+                @pl.when(p > 0)
+                def _():
+                    start(factors(p + d, 0))
+
+                start(factors_mate(p + d, x))
+
+    def starts_of():
+        begin, found = jnp.int32(0), []
+        for n in range(lengths.shape[1]):
+            found.append(begin)
+            begin = begin + lengths[0, n]
+        return found
+
+    def slots():
+        token = lax.broadcasted_iota(jnp.int32, (1, TOK), 1)
+        which = jnp.zeros((1, TOK), jnp.int32)
+        for n, begin in enumerate(starts_of()):
+            which = jnp.where(token >= begin, adapter_slot[request_adapter[0, n]], which)
+        return which
 
     def low_copy(owner, m):
         return remote(lr.at[owner], lr.at[owner], lsend.at[m], lrecv.at[owner], row=(r + m) % nr)
 
     def lowrank_start():
-        @pl.loop(1, nc)
-        def _(m):
-            down_copy((c + m) % nc, m).wait_recv()
+        @pl.loop(0, nb)
+        def _(b):
+            factors_mate(b, other)[0].wait_recv()
 
         everything = lax.dot_general(
             dn[...].reshape(nc * 2 * rank, raw.shape[1]), raw[...],
             (((1,), (1,)), ((), ())), preferred_element_type=F32)
-        which = slot[...]
+        which = slots()
         mine = jnp.zeros((2 * rank, TOK), F32)
         for a in range(nc):
             mine = mine + jnp.where(which == a, everything[a * 2 * rank:(a + 1) * 2 * rank], 0.0)
@@ -161,14 +239,14 @@
         def _(m):
             low_copy((r + m) % nr, m).wait_recv()
 
-        @pl.loop(1, nc)
-        def _(m):
-            up_copy((c + m) % nc, m).wait_recv()
+        @pl.loop(0, nb)
+        def _(b):
+            factors_mate(b, other)[1].wait_recv()
 
         total = lr[0]
         for o in range(1, nr):
             total = total + lr[o]
-        which = slot[...]
+        which = slots()
         for ref, part in ((sq, total[:rank]), (sv, total[rank:])):
             tall = jnp.concatenate([jnp.where(which == a, part, 0.0) for a in range(nc)], axis=0)
             ref[...] = tall.T.astype(BF16)
@@ -177,7 +255,11 @@
         @pl.loop(0, TOK // TILE)
         def _(i):
             rows = pl.ds(pl.multiple_of(i * TILE, TILE), TILE)
-            angle = pos[rows, :] * freq[...]
+            token = lax.broadcasted_iota(jnp.int32, (TILE, HEAD), 0) + i * TILE
+            position = token
+            for begin in starts_of():
+                position = jnp.where(token >= begin, token - begin, position)
+            angle = position.astype(F32) * freq[...]
             sign = jnp.where(lax.broadcasted_iota(jnp.int32, (TILE, HEAD), 1) < HEAD // 2, -1.0, 1.0)
             cosb[rows, :] = jnp.cos(angle)
             sinb[rows, :] = jnp.sin(angle) * sign
@@ -190,16 +272,18 @@
             total = term if total is None else total + term
         return total
 
-    def part_copy(j):
-        return remote(sendb.at[j], precv.at[j], psend.at[j], pget.at[j], col=mate)
+    def part_copy(j, h):
+        rows = slice(h * HALF, (h + 1) * HALF)
+        return remote(sendb.at[j, rows], precv.at[j, rows], psend.at[j, h], pget.at[j, h], col=mate)
 
     def compute(j):
-        @pl.loop(0, TOK // TILE)
-        def _(i):
-            rows = pl.ds(pl.multiple_of(i * TILE, TILE), TILE)
-            sendb[j, rows, :] = product(j, other, rows).astype(BF16)
-
-        part_copy(j).start()
+        for h in range(2):
+            @pl.loop(0, HALF // TILE)
+            def _(i):
+                rows = pl.ds(pl.multiple_of(h * HALF + i * TILE, TILE), TILE)
+                sendb[j, rows, :] = product(j, other, rows).astype(BF16)
+
+            part_copy(j, h).start()
 
         @pl.loop(0, TOK // TILE)
         def _(i):
@@ -207,11 +291,14 @@
             acc[j, rows, :] = product(j, x, rows)
 
     def combine(j):
-        part_copy(j).wait_recv()
-
-        @pl.loop(0, TOK // TILE)
+        for h in range(2):
+            part_copy(j, h).wait_recv()
+            combine_half(j, h)
+
+    def combine_half(j, h):
+        @pl.loop(0, HALF // TILE)
         def _(i):
-            rows = pl.ds(pl.multiple_of(i * TILE, TILE), TILE)
+            rows = pl.ds(pl.multiple_of(h * HALF + i * TILE, TILE), TILE)
             v = acc[j, rows, :] + precv[j, rows, :].astype(F32)
             if j >= 2:
                 at = (j - 2) * cw
@@ -235,16 +322,12 @@
     to_mate().start()
     spread_hidden(x)
     send_own(0)
-
-    @pl.loop(1, nc)
-    def _(m):
-        down_copy(c, m).start()
-        up_copy(c, m).start()
-
+    send_factors()
     for j in range(1, AHEAD):
         send_own(j)
     tables()
     service(0)
+    service_factors()
     from_mate().wait_recv()
     spread_hidden(other)
     pass_hidden(x)
@@ -283,7 +366,24 @@
             def _():
                 weight(b, j, 0).wait_send()
 
-        part_copy(j).wait_send()
+    for j in range(CHUNKS):
+        for h in range(2):
+            part_copy(j, h).wait_send()
+
+    @pl.loop(0, nb)
+    def _(b):
+        @pl.when((b <= p) & (p + 1 < nb))
+        def _():
+            for one in factors(b, 1):
+                one.wait_send()
+
+        @pl.when((b >= p) & (p > 0))
+        def _():
+            for one in factors(b, 0):
+                one.wait_send()
+
+        for one in factors_mate(b, x):
+            one.wait_send()
 
     to_mate().wait_send()
     for t in range(2):
@@ -292,79 +392,63 @@
         for m in range(nr // 2):
             to_twin((r + 2 * m) % nr, t).wait_send()
 
-    @pl.loop(1, nc)
-    def _(m):
-        down_copy(c, m).wait_send()
-        up_copy(c, m).wait_send()
-
     @pl.loop(1, nr)
     def _(m):
         low_copy(r, m).wait_send()
 
 
-def paging(table, first, count, kv, key, value):
-    n = pl.program_id(0)
+def paging(lengths, table, kv, key, value):
     window = PAGE + 16
     kw = key.shape[2]
-    base = pl.multiple_of(jnp.minimum(first[n] // 16 * 16, TOK - window), 16)
     row = lax.broadcasted_iota(jnp.int32, (PAGE, window), 0)
     column = lax.broadcasted_iota(jnp.int32, (PAGE, window), 1)
-    pick = ((column == row + (first[n] - base)) & (row < count[n])).astype(F32).astype(BF16)
-    rows = jnp.dot(pick, kv[pl.ds(base, window), :], preferred_element_type=F32).astype(BF16)
-    key[0] = rows[:, :kw]
-    value[0] = rows[:, kw:]
+    spans, begin, begin_page = [], jnp.int32(0), jnp.int32(0)
+    for n in range(lengths.shape[1]):
+        length = lengths[0, n]
+        spans.append((begin, begin_page, length))
+        begin = begin + length
+        begin_page = begin_page + (length + PAGE - 1) // PAGE
+    for number in range(key.shape[0]):
+        first, count = jnp.int32(0), jnp.int32(0)
+        for begin, begin_page, length in spans:
+            offset = (number - begin_page) * PAGE
+            inside = (offset >= 0) & (offset < length)
+            first = jnp.where(inside, begin + offset, first)
+            count = jnp.where(inside, jnp.minimum(length - offset, PAGE), count)
+        base = pl.multiple_of(jnp.minimum(first // 16 * 16, TOK - window), 16)
+        pick = ((column == row + (first - base)) & (row < count)).astype(F32).astype(BF16)
+        rows = jnp.dot(pick, kv[pl.ds(base, window), :], preferred_element_type=F32).astype(BF16)
+        page = table[0, number]
+        key[page] = rows[:, :kw]
+        value[page] = rows[:, kw:]
 
 
 def shards(nc, nr, hidden, w_query, w_key, w_value, adapter_down, adapter_up_query,
            adapter_up_value, lengths, request_adapter, adapter_slot, page_table):
     kb = w_query.shape[0]
     qw, kw = w_query.shape[1], w_key.shape[1]
-    width = qw + 2 * kw
-    cw = width // CHUNKS
+    cw = (qw + 2 * kw) // CHUNKS
     hw = hidden.shape[1]
     rank = adapter_up_query.shape[1]
     pages = page_table.shape[1]
     nb = nc // 2
 
-    lengths, page_row = lengths[0], page_table[0]
-    starts = jnp.cumsum(lengths) - lengths
-    token = jnp.arange(TOK, dtype=jnp.int32)
-    after = token[:, None] >= starts[None, :]
-    within = after & (token[:, None] < (starts + lengths)[None, :])
-    position = token - jnp.max(jnp.where(after, starts[None, :], 0), axis=1)
-    adapters = jnp.arange(nc, dtype=jnp.int32)
-    chosen_request = jnp.sum(
-        jnp.where(request_adapter[0][:, None] == adapters[None, :], adapter_slot[None, :], 0), axis=1)
-    chosen = jnp.sum(jnp.where(within, chosen_request[None, :], 0), axis=1)
-    frequency = jnp.exp(jnp.arange(HEAD // 2, dtype=F32) * (-2.0 * math.log(10000.0) / HEAD))
-    frequency = jnp.concatenate([frequency, frequency])[None, :]
-
-    pages_each = (lengths + PAGE - 1) // PAGE
-    page_start = jnp.cumsum(pages_each) - pages_each
-    number = jnp.arange(pages, dtype=jnp.int32)
-    started = number[:, None] >= page_start[None, :]
-    owner = jnp.sum(started.astype(jnp.int32), axis=1) - 1
-    mine = owner[:, None] == jnp.arange(lengths.shape[0], dtype=jnp.int32)[None, :]
-    offset = (number - jnp.sum(jnp.where(mine, page_start[None, :], 0), axis=1)) * PAGE
-    first = jnp.minimum(jnp.sum(jnp.where(mine, starts[None, :], 0), axis=1) + offset, TOK - 1)
-    count = jnp.clip(jnp.sum(jnp.where(mine, lengths[None, :], 0), axis=1) - offset, 0, PAGE)
-
-    w = jnp.concatenate([w_key, w_query, w_value], axis=1)
-    w = w.reshape(kb, CHUNKS, cw).transpose(1, 0, 2)
-    h2 = hidden.reshape(TOK, hw // (2 * kb), 2, kb).transpose(2, 0, 1, 3).reshape(2, TOK, hw // 2)
+    frequency = np.exp(np.arange(HEAD // 2) * (-2.0 * math.log(10000.0) / HEAD))
+    frequency = jnp.asarray(np.concatenate([frequency, frequency])[None, :], F32)
     down = adapter_down[0].T
-    up = jnp.concatenate([adapter_up_query[0], adapter_up_value[0]], axis=1)
 
     hbm = pl.BlockSpec(memory_space=pl.ANY)
     vmem = pl.BlockSpec(memory_space=pltpu.VMEM)
+    smem = pl.BlockSpec(memory_space=pltpu.SMEM)
     dma = pltpu.SemaphoreType.DMA
     query, kv = pl.pallas_call(
         functools.partial(project, nc, nr),
         out_shape=(jax.ShapeDtypeStruct((TOK, qw), BF16), jax.ShapeDtypeStruct((TOK, 2 * kw), BF16)),
-        in_specs=[hbm, hbm, vmem, hbm, hbm, vmem, vmem, vmem],
+        in_specs=[vmem, hbm, hbm, hbm, hbm, hbm, hbm, vmem, smem, smem, smem],
         out_specs=(vmem, vmem),
         scratch_shapes=[
             pltpu.VMEM((nb, CHUNKS, kb, cw), BF16),
+            pltpu.VMEM((2, TOK, hw // 2), BF16),
             pltpu.VMEM((nr, 2, TOK, hw // 2), BF16),
             pltpu.VMEM((CHUNKS, TOK, cw), F32),
             pltpu.VMEM((CHUNKS, TOK, cw), BF16),
@@ -376,7 +460,8 @@
             pltpu.VMEM((TOK, nc * rank), BF16),
             pltpu.VMEM((TOK, HEAD), F32),
             pltpu.VMEM((TOK, HEAD), F32),
-            dma((4,)),
+            dma((CHUNKS,)),
+            dma((3,)),
             dma((2, nb, CHUNKS)),
             dma((nb, CHUNKS)),
             dma((2, nr)),
@@ -384,11 +469,13 @@
             dma((nr, 2)),
             dma,
             dma,
-            dma((CHUNKS,)),
-            dma((CHUNKS,)),
+            dma((CHUNKS, 2)),
+            dma((CHUNKS, 2)),
+            dma((2, nb)),
+            dma((nb,)),
             dma((nc,)),
-            dma((nc,)),
-            dma((nc,)),
+            dma((2, nb)),
+            dma((nb,)),
             dma((nc,)),
             dma((nr,)),
             dma((nr,)),
@@ -396,20 +483,17 @@
         compiler_params=pltpu.CompilerParams(
             collective_id=0, has_side_effects=True, vmem_limit_bytes=60 * 1024 * 1024),
         name="project",
-    )(h2, w, hidden, down, up, position.astype(F32)[:, None], chosen[None, :], frequency)
+    )(hidden, w_query, w_key, w_value, down, adapter_up_query, adapter_up_value, frequency,
+      lengths, request_adapter, adapter_slot)
 
     key_cache, value_cache = pl.pallas_call(
         paging,
         out_shape=(jax.ShapeDtypeStruct((pages, PAGE, kw), BF16),) * 2,
-        grid_spec=pltpu.PrefetchScalarGridSpec(
-            num_scalar_prefetch=3,
-            grid=(pages,),
-            in_specs=[pl.BlockSpec((TOK, 2 * kw), lambda n, table, first, count: (0, 0))],
-            out_specs=[pl.BlockSpec((1, PAGE, kw), lambda n, table, first, count: (table[n], 0, 0))] * 2,
-        ),
+        in_specs=[smem, smem, vmem],
+        out_specs=(vmem, vmem),
         compiler_params=pltpu.CompilerParams(vmem_limit_bytes=32 * 1024 * 1024),
         name="paging",
-    )(page_row, first, count, kv)
+    )(lengths, page_table, kv)
     return (query, key_cache, value_cache)
 
 

time: 234 us -> 200 us (0.85)
  Pallas kernels: 214 us -> 197 us
  other arithmetic: 8.43 us -> 0 us
  local copies, waits for them, and re-layouts: 10.1 us -> 2.92 us
    pallas_call x1, Pallas kernels: 206 us -> 192 us  [shards(): pl.pallas_call(functools.partial(project, nc, nr), out_shape=(jax.ShapeDt...]
    pallas_call x1, Pallas kernels: 8.76 us -> 4.17 us  [shards(): pl.pallas_call(paging, out_shape=(jax.ShapeDtypeStruct((pages, PAGE, kw),...]
    reshape x2 -> x0, local copies, waits for them, and re-layouts: 4.14 us -> none  [the longest x1 2.58 us: shards(): hidden.reshape(TOK, hw // (2 * kb), 2, kb).transpose(2, 0, 1, 3)]
    concatenate x2 -> x0, other arithmetic: 2.9 us -> none  [the longest x1 1.5 us: shards(): w = jnp.concatenate([w_key, w_query, w_value], axis=1)]
    unnamed x10 -> x9, local copies, waits for them, and re-layouts: 5.75 us -> 2.92 us
where the time goes in v2:
time: 200 us
  Pallas kernels  197 us (98%)
  local copies, waits for them, and re-layouts  2.92 us (1%)
    pallas_call x1, Pallas kernels, shards(): pl.pallas_call(functools.partial(project, nc, nr), out_shape=(jax.ShapeDt...  192 us
    pallas_call x1, Pallas kernels, shards(): pl.pallas_call(paging, out_shape=(jax.ShapeDtypeStruct((pages, PAGE, kw),...  4.17 us

profile of v2, /device:TPU:0, one launch (start us, length us, event | category | flops | bytes accessed | tf_op | source)
XLA Modules:
  0.0 200.2 jit_solution(6825611123268098875)
XLA Ops:
  0.6 0.0 copy-start.1
  0.6 0.0 copy-start.2
  0.7 192.5 %project.1 = (bf16[1024,1024]{1,0:T(8,128)(2,1)}, bf16[1024,1024]{1,0:T(8,128)(2,1)}) custom-call(bf16[1024,1152]{1,0:T(8,128)(2,1)} %raw.1, bf16[576,1024]{1,0:T(8,128)(2,1)} %w_query.1, bf16[576,512]{1,0:T(8,128)(2,1)} %w_key.1, bf16[576,512]{1,0:T(8,128)(2,1)} %w_value.1, bf16[32,1152]{1,0:T(8,128)(2,1)} %bitcast.3, bf16[1,16,1024]{2,1,0:T(8,128)(2,1)} %upq_in.1, ...), custom_call_target="tpu_custom_call" | custom-call | tf_op jit(solution)/shard_map/project/pallas_call | solution.py:444
  193.1 0.0 copy-done.1
  193.1 0.0 copy-done.2
  193.1 0.0 copy-start
  193.2 1.6 copy-done
  194.7 0.0 copy-start.3
  194.7 4.2 %paging.1 = (bf16[18,128,512]{2,1,0:T(8,128)(2,1)}, bf16[18,128,512]{2,1,0:T(8,128)(2,1)}) custom-call(s32[1,10]{1,0:T(1,128)S(1)} %copy-done.1, s32[1,18]{1,0:T(1,128)S(1)} %copy-done.2, bf16[1024,1024]{1,0:T(8,128)(2,1)S(1)} %copy-done), custom_call_target="tpu_custom_call" | custom-call | tf_op jit(solution)/shard_map/paging/pallas_call | solution.py:489
  198.9 0.0 copy-done.3
  198.9 1.3 copy.16
Async XLA Ops:
  0.6 192.5 %copy-start.1 = (s32[1,10]{1,0:T(1,128)S(1)}, s32[1,10]{1,0:T(1,128)}, u32[]{:S(2)}) copy-start(s32[1,10]{1,0:T(1,128)} %lengths.3) | copy-start | bytes 124
  0.6 192.5 %copy-start.2 = (s32[1,18]{1,0:T(1,128)S(1)}, s32[1,18]{1,0:T(1,128)}, u32[]{:S(2)}) copy-start(s32[1,18]{1,0:T(1,128)} %table.1) | copy-start | bytes 220
  193.1 1.6 copy-start
  194.7 4.2 %copy-start.3 = (bf16[1024,1024]{1,0:T(8,128)(2,1)S(1)}, bf16[1024,1024]{1,0:T(8,128)(2,1)}, u32[]{:S(2)}) copy-start(bf16[1024,1024]{1,0:T(8,128)(2,1)} %get-tuple-element.14) | copy-start | bytes 6291460
